TPU v7x, 32 devices: a whole 2x2x4 slice. The times are simulated.
32 devices in a mesh: sec: 4 (over y, x), lat: 8 (over z, core).
Axes of the slice: x: 2, y: 2, z: 4, core: 2. Of those that a mesh axis runs over, the one named last changes fastest.
Arguments:
- states: float32 [4, 3, 448, 4096], P('sec', None, 'lat'), may hold values from -40 to 40
- depth_field: float32 [448, 4096], P('lat'), may hold values from 0.07 to 1
- land_mask: int32 [448, 4096], P('lat'), may hold values 0 or 1
- tide_cos: float32 [448, 4096], P('lat'), may hold values from -8 to 8
- tide_sin: float32 [448, 4096], P('lat'), may hold values from -8 to 8
Outputs:
- new_states: float32 [4, 3, 448, 4096], P('sec', None, 'lat')
- mismatch: float32 [4, 3, 448, 4096], P('sec', None, 'lat')
- step_length: float32 [], replicated
All inputs are finite; a program needn't handle non-finite values. No bound on the sum of `land_mask` on one device may be relied on, other than what follows from the above.
Results may differ from a plain program's by a relative error of at most 0.00002.
Values sent between devices are 32-bit elements; how exact they have to be, the bound alone decides.
A program may use at most 64 MiB of HBM per device.

v0:
```python
import functools
import math

import jax
import jax.numpy as jnp
import numpy as np
from jax import lax
from jax.experimental import pallas as pl
from jax.experimental.pallas import tpu as pltpu
from jax.sharding import PartitionSpec as P

STEPS = 4
DRAG_RATE = 0.9
CORIOLIS_MAX = 0.3
EPSILON = 1e-06
TWO_PI = 2.0 * math.pi
HALO = 24
STRIPS = 7
MESH = pl.DeviceIdType.MESH


def kernel(
    sections, bands, count,
    states, depth, mask, tide_one, tide_two, rows_in, trig,
    home, full, step_out,
    wide, mask_win, st, start, mis, grad,
    high, east, north, raised, flux, fluy, acc, part, total,
    load_sem, s1, r1, halo_s, halo_r, st_s, st_r, s2, r2, s3, r3, own_sem, ps, pr, ts, tr,
):
    me = lax.axis_index("sec")
    band = lax.axis_index("lat")
    rows, lon = states.shape[1], states.shape[2]
    share = lon // sections
    per, tiles = share // 128, lon // 128
    wins = per + 1
    tall = rows + 2 * HALO
    strips = tall // 8
    top, low = HALO, HALO + rows

    def peer(i):
        return lax.rem(me + i, sections)

    def tile(c):
        return pl.ds(pl.multiple_of(c * 128, 128), 128)

    def load_states(c, _):
        src = states.at[:, :, tile(c)]
        pltpu.make_async_copy(src, wide.at[c + c // per], load_sem.at[0]).start()
        return 0

    lax.fori_loop(0, tiles, load_states, 0)
    singles = (
        (depth, st.at[0, :, pl.ds(top, rows)]),
        (mask, mask_win),
        (tide_one, st.at[2, :, pl.ds(top, rows)]),
        (tide_two, st.at[3, :, pl.ds(top, rows)]),
    )

    def load_static(c, _):
        ahead = jnp.where(c == wins, tiles - 1, c)
        at = tile(lax.rem(me * per + ahead, tiles))
        for n, (src, dst) in enumerate(singles):
            pltpu.make_async_copy(src.at[:, at], dst.at[c], load_sem.at[1 + n]).start()
        return 0

    lax.fori_loop(0, wins + 1, load_static, 0)

    barrier = pltpu.get_barrier_semaphore()
    for i in range(1, sections):
        pl.semaphore_signal(barrier, inc=1, device_id={"sec": peer(i)}, device_id_type=MESH)
    for i in range(1, bands):
        pl.semaphore_signal(
            barrier, inc=1, device_id={"lat": lax.rem(band + i, bands)}, device_id_type=MESH
        )
    pl.semaphore_wait(barrier, sections + bands - 2)

    loaded = wide.at[pl.ds(0, tiles)]
    pltpu.make_async_copy(loaded, loaded, load_sem.at[0]).wait()
    early = lax.broadcasted_iota(jnp.int32, (8, 128), 1) < 64

    def pack(r, _):
        at = pl.ds(pl.multiple_of(8 * r, 8), 8)
        for j in range(sections):
            after, before = (j + 1) % sections * wins, (j - 1) % sections * wins + per - 1
            for a in range(3):
                wide[j * wins + per, a, at, :] = jnp.where(
                    early, wide[after, a, at, :], wide[before, a, at, :]
                )
        return 0

    lax.fori_loop(0, rows // 8, pack, 0)

    def piece(j, slot):
        return pltpu.make_async_remote_copy(
            src_ref=wide.at[pl.ds(j * wins, wins)],
            dst_ref=start.at[me, :, :, pl.ds(top, rows), :],
            send_sem=s1.at[j],
            recv_sem=r1.at[slot],
            device_id={"sec": j},
            device_id_type=MESH,
        )

    def turn(n):
        return lax.rem(me + jnp.where(lax.rem(me, 2) == 0, n, sections - n), sections)

    for n in range(1, sections - 1):
        piece(turn(n), me).start()
    own = pltpu.make_async_copy(
        wide.at[pl.ds(me * wins, wins)],
        start.at[me, :, :, pl.ds(top, rows), :],
        own_sem.at[0],
    )
    own.start()

    up_ok, down_ok = band > 0, band < bands - 1

    def to_above(s):
        return pltpu.make_async_remote_copy(
            src_ref=start.at[s, :, :, pl.ds(top, HALO), :],
            dst_ref=start.at[s, :, :, pl.ds(low, HALO), :],
            send_sem=halo_s.at[0, s], recv_sem=halo_r.at[0, s],
            device_id={"lat": band - 1}, device_id_type=MESH,
        )

    def to_below(s):
        return pltpu.make_async_remote_copy(
            src_ref=start.at[s, :, :, pl.ds(low - HALO, HALO), :],
            dst_ref=start.at[s, :, :, pl.ds(0, HALO), :],
            send_sem=halo_s.at[1, s], recv_sem=halo_r.at[1, s],
            device_id={"lat": band + 1}, device_id_type=MESH,
        )

    def st_above():
        return pltpu.make_async_remote_copy(
            src_ref=st.at[:, pl.ds(0, wins), pl.ds(top, HALO), :], dst_ref=st.at[:, pl.ds(0, wins), pl.ds(low, HALO), :],
            send_sem=st_s.at[0], recv_sem=st_r.at[0],
            device_id={"lat": band - 1}, device_id_type=MESH,
        )

    def st_below():
        return pltpu.make_async_remote_copy(
            src_ref=st.at[:, pl.ds(0, wins), pl.ds(low - HALO, HALO), :], dst_ref=st.at[:, pl.ds(0, wins), pl.ds(0, HALO), :],
            send_sem=st_s.at[1], recv_sem=st_r.at[1],
            device_id={"lat": band + 1}, device_id_type=MESH,
        )

    def send_halo(s):
        @pl.when(up_ok)
        def _():
            to_above(s).start()

        @pl.when(down_ok)
        def _():
            to_below(s).start()

    def recv_halo(s):
        @pl.when(down_ok)
        def _():
            to_above(s).wait_recv()

        @pl.when(up_ok)
        def _():
            to_below(s).wait_recv()

    own.wait()
    send_halo(me)

    for n, (src, dst) in enumerate(singles):
        pltpu.make_async_copy(dst, dst, load_sem.at[1 + n]).wait()

    def prepare(r, _):
        at = pl.ds(pl.multiple_of(top + 8 * r, 8), 8)
        for c in range(wins + 1):
            sea = mask_win[c, pl.ds(pl.multiple_of(8 * r, 8), 8), :].astype(jnp.float32)
            st[1, c, at, :] = sea
            st[0, c, at, :] = st[0, c, at, :] * sea
        for a in range(4):
            st[a, per, at, :] = jnp.where(early, st[a, per, at, :], st[a, wins, at, :])
        return 0

    lax.fori_loop(0, rows // 8, prepare, 0)

    @pl.when(up_ok)
    def _():
        st_above().start()

    @pl.when(down_ok)
    def _():
        st_below().start()

    zero = jnp.zeros((8, 128), jnp.float32)

    def blank(first):
        def body(r, _):
            at = pl.ds(pl.multiple_of(first + 8 * r, 8), 8)
            for c in range(wins):
                for a in range(4):
                    st[a, c, at, :] = zero
                for s in range(sections):
                    for a in range(3):
                        start[s, c, a, at, :] = zero
            return 0

        lax.fori_loop(0, HALO // 8, body, 0)

    @pl.when(band == 0)
    def _():
        blank(0)

    @pl.when(band == bands - 1)
    def _():
        blank(low)

    def edge(lo, hi):
        for buf in (raised, flux):
            for c in range(wins):
                buf[c, pl.ds(8 * lo, 8), :] = zero
                buf[c, pl.ds(8 * hi + 8, 8), :] = zero

    acc[...] = jnp.zeros_like(acc)

    @pl.when(down_ok)
    def _():
        st_above().wait_recv()

    @pl.when(up_ok)
    def _():
        st_below().wait_recv()

    def lon_diff(xs, c):
        lane = lax.broadcasted_iota(jnp.int32, xs[c].shape, 1)
        after, before = xs[(c + 1) % wins], xs[c - 1]
        east_of = pltpu.roll(jnp.where(lane == 0, after, xs[c]), 127, 1)
        return east_of - pltpu.roll(jnp.where(lane == 127, before, xs[c]), 1, 1)

    def lon_diffs(xs):
        return [lon_diff(xs, c) for c in range(wins)]

    def lat_diff(ref, c, r0, high):
        return ref[c, pl.ds(r0 + 9, high), :] - ref[c, pl.ds(r0 + 7, high), :]

    def sweep(lo, hi, body):
        n = -(-(hi - lo) // STRIPS)
        size, more = divmod(hi - lo, n)
        at = lo
        for length, times in ((size + 1, more), (size, n - more)):
            if times:
                def turns(i, _, at=at, length=length):
                    r0 = pl.multiple_of(8 * (at + i * length), 8)
                    body(r0, 8 * length, pl.ds(r0, 8 * length), pl.ds(pl.multiple_of(r0 + 8, 8), 8 * length))
                    return 0

                lax.fori_loop(0, times, turns, 0)
                at += length * times

    def strip_sum(xs):
        return jnp.sum(sum(xs).reshape(-1, 8, 128), axis=0)

    def run(kind, source, s, lo, hi, finish, target_of=None):
        def push(h, c, at, step):
            if kind != "forced":
                return 0.5 * h
            base = 2 * (s * STEPS + step)
            return 0.5 * (h + (trig[base] * st[2, c, at, :] + trig[base + 1] * st[3, c, at, :]))

        def begin(r0, high_rows, at, padded):
            for c in range(wins):
                raised[c, padded, :] = push(source[s, c, 0, at, :], c, at, 0)

        sweep(lo, hi, begin)
        edge(lo, hi)

        def advance(step, is_first, is_last):
            def first(r0, high_rows, at, padded):
                slopes = lon_diffs([raised[c, padded, :] for c in range(wins)])
                cor = rows_in[0, at, :]
                for c in range(wins):
                    wet, sea = st[0, c, at, :], st[1, c, at, :]
                    dx, dy = slopes[c], lat_diff(raised, c, r0, high_rows)
                    if is_first:
                        u, v = source[s, c, 1, at, :], source[s, c, 2, at, :]
                    else:
                        u, v = east[c, at, :], north[c, at, :]
                    if kind == "back":
                        e = sea * (u + wet * dx)
                        f = sea * (v + wet * dy)
                        east[c, at, :] = DRAG_RATE * e - cor * f
                        north[c, at, :] = cor * e + DRAG_RATE * f
                        fluy[c, at, :], flux[c, padded, :] = 0.5 * e, 0.5 * f
                    else:
                        e = sea * (DRAG_RATE * u + cor * v - dx)
                        f = sea * (DRAG_RATE * v - cor * u - dy)
                        half = 0.5 * wet
                        east[c, at, :], north[c, at, :] = e, f
                        fluy[c, at, :], flux[c, padded, :] = half * e, half * f

            sweep(lo, hi, first)

            def second(r0, high_rows, at, padded):
                slopes = lon_diffs([fluy[c, at, :] for c in range(wins)])
                inside = rows_in[1, at, :]
                sums = []
                for c in range(wins):
                    d = slopes[c] + lat_diff(flux, c, r0, high_rows)
                    h = source[s, c, 0, at, :] if is_first else high[c, at, :]
                    h = (h + d if kind == "back" else h - d) * inside
                    if not is_last:
                        high[c, at, :], raised[c, padded, :] = h, push(h, c, at, step + 1)
                        continue
                    values = finish(c, at, (h, east[c, at, :], north[c, at, :]))
                    if kind == "free":
                        if c < per:
                            sums.append(values)
                    else:
                        target, slot = target_of
                        for a in range(3):
                            target[slot, c, a, at, :] = values[a]
                if sums:
                    acc[0] += strip_sum([x for x, _ in sums])
                    acc[1] += strip_sum([x for _, x in sums])

            inner = 1 if is_last else 0
            sweep(lo + inner, hi - inner, second)

        advance(0, True, False)

        def middle(step, _):
            advance(step, False, False)
            return 0

        lax.fori_loop(1, STEPS - 1, middle, 0)
        advance(STEPS - 1, False, True)

    def keep(c, at, values):
        return values

    def arrive(n):
        s = turn(n)
        piece(s, s).wait_recv()
        send_halo(s)

    def forced(n, _):
        @pl.when(n == 1)
        def _():
            for i in range(1, sections - 1):
                piece(turn(i), me).wait_send()
            piece(turn(sections - 1), me).start()
            for i in range(1, sections - 1):
                arrive(i)

        @pl.when(n == sections - 2)
        def _():
            arrive(sections - 1)

        s = turn(n)
        recv_halo(s)
        run("forced", start, s, 0, strips, keep, (mis, s))
        return 0

    lax.fori_loop(0, sections, forced, 0)

    def subtract(s, after):
        def body(r, _):
            at = pl.ds(pl.multiple_of(8 * r, 8), 8)
            out = [
                [mis[s, c, a, at, :] - start[after, c, a, at, :] for a in range(3)]
                for c in range(wins)
            ]
            for c in range(wins):
                for a in range(3):
                    mis[s, c, a, at, :] = out[c][a]
            return 0

        lax.fori_loop(1, strips - 1, body, 0)

    subtract(me, peer(1))
    columns = pl.ds(me * per, per)
    own_mis = pltpu.make_async_copy(
        mis.at[me, pl.ds(0, per), :, pl.ds(top, rows), :],
        home.at[columns],
        own_sem.at[1],
    )
    own_mis.start()

    def give(source, target, send, recv, s, at_columns, slot):
        return pltpu.make_async_remote_copy(
            src_ref=source.at[s, pl.ds(0, per), :, pl.ds(top, rows), :],
            dst_ref=target.at[at_columns],
            send_sem=send.at[s], recv_sem=recv.at[slot],
            device_id={"sec": s}, device_id_type=MESH,
        )

    def differ(i, _):
        s = peer(i)
        subtract(s, peer(i + 1))
        give(mis, home, s2, r2, s, columns, me).start()
        return 0

    lax.fori_loop(1, sections, differ, 0)

    def back(i, _):
        s = peer(i)
        before = peer(i + sections - 1)

        def done(c, at, values):
            return [x - mis[before, c, a, at, :] for a, x in enumerate(values)]

        run("back", mis, s, 1, strips - 1, done, (grad, s))

        @pl.when(i < sections)
        def _():
            give(grad, full, s3, r3, s, columns, me).start()

        return 0

    lax.fori_loop(1, sections + 1, back, 0)
    own_grad = pltpu.make_async_copy(
        grad.at[me, pl.ds(0, per), :, pl.ds(top, rows), :],
        full.at[columns],
        own_sem.at[2],
    )
    own_grad.start()

    def image(i, _):
        s = peer(i)
        after = peer(i + 1)

        def squares(c, at, values):
            pairs = [(x, grad[after, c, a, at, :]) for a, x in enumerate(values)]
            return sum(g * g for _, g in pairs), sum((x - g) * (x - g) for x, g in pairs)

        run("free", grad, s, 2, strips - 2, squares)
        return 0

    lax.fori_loop(0, sections, image, 0)

    part[me] = acc[...]

    def share_part(j, slot):
        return pltpu.make_async_remote_copy(
            src_ref=acc, dst_ref=part.at[slot], send_sem=ps.at[j], recv_sem=pr.at[slot],
            device_id={"sec": j}, device_id_type=MESH,
        )

    for i in range(1, sections):
        share_part(peer(i), me).start()
    for i in range(1, sections):
        share_part(peer(i), peer(i)).wait_recv()
    for i in range(1, sections):
        share_part(peer(i), me).wait_send()
    summed = part[0]
    for s in range(1, sections):
        summed = summed + part[s]
    acc[...] = summed
    total[band] = summed

    def share_total(j, slot):
        return pltpu.make_async_remote_copy(
            src_ref=acc, dst_ref=total.at[slot], send_sem=ts.at[j], recv_sem=tr.at[slot],
            device_id={"lat": j}, device_id_type=MESH,
        )

    for i in range(1, bands):
        share_total(lax.rem(band + i, bands), band).start()
    for i in range(1, bands):
        j = lax.rem(band + i, bands)
        share_total(j, j).wait_recv()
    summed = total[0]
    for s in range(1, bands):
        summed = summed + total[s]
    sums = jnp.sum(jnp.sum(summed, axis=2, keepdims=True), axis=1, keepdims=True)
    step = sums[0] / count / (sums[1] / count + EPSILON)
    step_out[...] = jnp.broadcast_to(step, (8, 128))

    own_mis.wait()

    def mismatches(i, _):
        s = peer(i)
        give(mis, home, s2, r2, s, columns, s).wait()
        return 0

    lax.fori_loop(1, sections, mismatches, 0)

    own_grad.wait()

    def grads(i, _):
        s = peer(i)
        give(grad, full, s3, r3, s, columns, s).wait_recv()
        return 0

    lax.fori_loop(1, sections, grads, 0)


    piece(turn(sections - 1), me).wait_send()

    def drain(i, _):
        s = peer(i)
        give(grad, full, s3, r3, s, columns, me).wait_send()
        return 0

    lax.fori_loop(1, sections, drain, 0)

    def drain_halo(i, _):
        s = peer(i)

        @pl.when(up_ok)
        def _():
            to_above(s).wait_send()

        @pl.when(down_ok)
        def _():
            to_below(s).wait_send()

        return 0

    lax.fori_loop(0, sections, drain_halo, 0)

    @pl.when(up_ok)
    def _():
        st_above().wait_send()

    @pl.when(down_ok)
    def _():
        st_below().wait_send()

    for i in range(1, bands):
        share_total(lax.rem(band + i, bands), band).wait_send()


def finish_kernel(fields, home, full, step, new_fields, mismatch):
    rows, share = fields.shape[1:]
    length = step[0:1, :]

    def body(r, _):
        at = pl.ds(pl.multiple_of(8 * r, 8), 8)
        for c in range(share // 128):
            cols = slice(c * 128, c * 128 + 128)
            for a in range(3):
                new_fields[a, at, cols] = fields[a, at, cols] - length * full[c, a, at, :]
                mismatch[a, at, cols] = home[c, a, at, :]
        return 0

    lax.fori_loop(0, rows // 8, body, 0)


def shards(states, depth_field, land_mask, tide_cos, tide_sin):
    fields = states[0]
    rows, lon = fields.shape[1:]
    sections, bands = lax.axis_size("sec"), lax.axis_size("lat")
    band = lax.axis_index("lat")
    share = lon // sections
    tall = rows + 2 * HALO
    lat_total = rows * bands
    ids = band * rows - HALO + jnp.arange(tall, dtype=jnp.int32)
    inside = ((ids >= 0) & (ids < lat_total)).astype(jnp.float32)
    coriolis = CORIOLIS_MAX * jnp.sin(
        jnp.pi * (ids.astype(jnp.float32) + 0.5) / lat_total - 0.5 * jnp.pi
    )
    rows_in = jnp.broadcast_to(jnp.stack([coriolis, inside])[:, :, None], (2, tall, 128))
    angles = np.float32(TWO_PI) * np.arange(sections * STEPS, dtype=np.float32) / np.float32(
        sections * STEPS
    )
    trig = jnp.asarray(np.stack([np.cos(angles), np.sin(angles)], axis=1).reshape(-1))
    f32 = jnp.float32
    dma = pltpu.SemaphoreType.DMA
    any_spec = pl.BlockSpec(memory_space=pl.ANY)
    vmem = pl.BlockSpec(memory_space=pltpu.VMEM)
    tiles, wins = lon // 128, share // 128 + 1
    stacked = pltpu.VMEM((sections, wins, 3, tall, 128), f32)
    plain = pltpu.VMEM((wins, tall, 128), f32)
    padded = pltpu.VMEM((wins, tall + 16, 128), f32)
    gathered = jax.ShapeDtypeStruct((tiles, 3, rows, 128), f32)
    home, full, step = pl.pallas_call(
        functools.partial(kernel, sections, bands, float(sections * 3 * lat_total * lon)),
        out_shape=(
            gathered,
            gathered,
            jax.ShapeDtypeStruct((8, 128), f32),
        ),
        in_specs=[any_spec] * 5 + [vmem, pl.BlockSpec(memory_space=pltpu.SMEM)],
        out_specs=(any_spec, any_spec, vmem),
        scratch_shapes=[
            pltpu.VMEM((tiles + sections, 3, rows, 128), f32),
            pltpu.VMEM((wins + 1, rows, 128), jnp.int32),
            pltpu.VMEM((4, wins + 1, tall, 128), f32),
            stacked, stacked, stacked,
            plain, plain, plain, padded, padded, plain,
            pltpu.VMEM((2, 8, 128), f32),
            pltpu.VMEM((sections, 2, 8, 128), f32),
            pltpu.VMEM((bands, 2, 8, 128), f32),
            dma((5,)),
            dma((sections,)), dma((sections,)),
            dma((2, sections)), dma((2, sections)),
            dma((2,)), dma((2,)),
            dma((sections,)), dma((sections,)),
            dma((sections,)), dma((sections,)),
            dma((3,)),
            dma((sections,)), dma((sections,)),
            dma((bands,)), dma((bands,)),
        ],
        compiler_params=pltpu.CompilerParams(
            collective_id=0, has_side_effects=True, vmem_limit_bytes=60 * 1024 * 1024
        ),
        name="shooting",
    )(fields, depth_field, land_mask, tide_cos, tide_sin, rows_in, trig)
    block = pl.BlockSpec((3, rows, share), lambda i: (0, 0, i))
    by_tile = pl.BlockSpec((share // 128, 3, rows, 128), lambda i: (i, 0, 0, 0))
    new_fields, mismatch = pl.pallas_call(
        finish_kernel,
        grid=(sections,),
        out_shape=(jax.ShapeDtypeStruct(fields.shape, f32),) * 2,
        in_specs=[block, by_tile, by_tile, pl.BlockSpec((8, 128), lambda i: (0, 0))],
        out_specs=(block, block),
        compiler_params=pltpu.CompilerParams(vmem_limit_bytes=32 * 1024 * 1024),
        name="update",
    )(fields, home, full, step)
    return new_fields[None], mismatch[None], step[0, 0]


def solution(mesh):
    return jax.shard_map(
        shards,
        mesh=mesh,
        in_specs=(
            P("sec", None, "lat", None),
            P("lat", None),
            P("lat", None),
            P("lat", None),
            P("lat", None),
        ),
        out_specs=(P("sec", None, "lat", None), P("sec", None, "lat", None), P()),
        check_vma=False,
    )
```

profile of v0, /device:TPU:0, one launch (start us, length us, event | category | flops | bytes accessed | tf_op | source)
XLA Modules:
  0.0 125.7 jit_solution(16552467722425316809)
XLA Ops:
  0.7 0.7 broadcast_in_dim.12.rows_in
  1.5 0.0 copy-start
  1.5 116.4 %shooting.1 = (f32[32,3,56,128]{3,2,1,0:T(8,128)}, f32[32,3,56,128]{3,2,1,0:T(8,128)}, f32[8,128]{1,0:T(8,128)}) custom-call(f32[3,56,4096]{2,1,0:T(8,128)} %bitcast.4, f32[56,4096]{1,0:T(8,128)} %depth.1, s32[56,4096]{1,0:T(8,128)} %mask.1, f32[56,4096]{1,0:T(8,128)} %tide_one.1, f32[56,4096]{1,0:T(8,128)} %tide_two.1, ...), custom_call_target="tpu_custom_call" | custom-call | tf_op jit(solution)/shard_map/shooting/pallas_call | solution.py:573
  117.9 0.0 copy-done
  117.9 0.0 copy-start.1
  117.9 1.8 %copy-done.1 = f32[32,3,56,128]{3,2,1,0:T(8,128)S(1)} copy-done((f32[32,3,56,128]{3,2,1,0:T(8,128)S(1)}, f32[32,3,56,128]{3,2,1,0:T(8,128)}, u32[]{:S(2)}) %copy-start.1) | copy-done | bytes 2752536
  119.7 0.0 copy-start.2
  119.7 1.8 %copy-done.2 = f32[32,3,56,128]{3,2,1,0:T(8,128)S(1)} copy-done((f32[32,3,56,128]{3,2,1,0:T(8,128)S(1)}, f32[32,3,56,128]{3,2,1,0:T(8,128)}, u32[]{:S(2)}) %copy-start.2) | copy-done | bytes 2752536
  121.5 0.0 copy-start.3
  121.5 0.7 copy-done.3
  122.1 3.1 %update.1 = (f32[3,56,4096]{2,1,0:T(8,128)}, f32[3,56,4096]{2,1,0:T(8,128)}) custom-call(f32[3,56,4096]{2,1,0:T(8,128)S(1)} %bitcast.5, f32[32,3,56,128]{3,2,1,0:T(8,128)S(1)} %copy-done.1, f32[32,3,56,128]{3,2,1,0:T(8,128)S(1)} %copy-done.2, f32[8,128]{1,0:T(8,128)S(1)} %copy-done.3), custom_call_target="tpu_custom_call" | custom-call | tf_op jit(solution)/shard_map/update/pallas_call | solution.py:608
  125.2 0.5 slice.3
  (3 shorter events, 0.1 us)
Async XLA Ops:
  1.5 116.4 %copy-start = (f32[1,3,56,4096]{3,2,1,0:T(8,128)S(1)}, f32[1,3,56,4096]{3,2,1,0:T(8,128)}, u32[]{:S(2)}) copy-start(f32[1,3,56,4096]{3,2,1,0:T(8,128)} %param.6) | copy-start | bytes 8257540
  117.9 1.8 %copy-start.1 = (f32[32,3,56,128]{3,2,1,0:T(8,128)S(1)}, f32[32,3,56,128]{3,2,1,0:T(8,128)}, u32[]{:S(2)}) copy-start(f32[32,3,56,128]{3,2,1,0:T(8,128)} %get-tuple-element.8.home) | copy-start | bytes 8257540
  119.7 1.8 %copy-start.2 = (f32[32,3,56,128]{3,2,1,0:T(8,128)S(1)}, f32[32,3,56,128]{3,2,1,0:T(8,128)}, u32[]{:S(2)}) copy-start(f32[32,3,56,128]{3,2,1,0:T(8,128)} %get-tuple-element.9.full) | copy-start | bytes 8257540
  121.5 0.7 copy-start.3
where the time goes:
time: 126 us
  Pallas kernels  119 us (94%)
  local copies, waits for them, and re-layouts  5.49 us (4%)
    pallas_call x1, Pallas kernels, shards(): pl.pallas_call(functools.partial(kernel, sections, bands, float(sections...  116 us
    unnamed x8, local copies, waits for them, and re-layouts  4.24 us
    pallas_call x1, Pallas kernels, shards(): pl.pallas_call(finish_kernel, grid=(sections,), out_shape=(jax.ShapeDtype...  3.07 us

commit v1 on v0

--- a/solution.py
+++ b/solution.py
@@ -21,9 +21,9 @@
 
 def kernel(
     sections, bands, count,
-    states, depth, mask, tide_one, tide_two, rows_in, trig,
+    states, depth, mask, tide_one, tide_two, row_table, trig,
     home, full, step_out,
-    wide, mask_win, st, start, mis, grad,
+    plain, plain_st, plain_mask, rows_in, wide, st, start, mis, grad,
     high, east, north, raised, flux, fluy, acc, part, total,
     load_sem, s1, r1, halo_s, halo_r, st_s, st_r, s2, r2, s3, r3, own_sem, ps, pr, ts, tr,
 ):
@@ -43,27 +43,20 @@
     def tile(c):
         return pl.ds(pl.multiple_of(c * 128, 128), 128)
 
-    def load_states(c, _):
-        src = states.at[:, :, tile(c)]
-        pltpu.make_async_copy(src, wide.at[c + c // per], load_sem.at[0]).start()
-        return 0
-
-    lax.fori_loop(0, tiles, load_states, 0)
+    pltpu.make_async_copy(states, plain, load_sem.at[0]).start()
     singles = (
-        (depth, st.at[0, :, pl.ds(top, rows)]),
-        (mask, mask_win),
-        (tide_one, st.at[2, :, pl.ds(top, rows)]),
-        (tide_two, st.at[3, :, pl.ds(top, rows)]),
+        (depth, plain_st.at[0]), (mask, plain_mask), (tide_one, plain_st.at[1]), (tide_two, plain_st.at[2])
     )
-
-    def load_static(c, _):
-        ahead = jnp.where(c == wins, tiles - 1, c)
-        at = tile(lax.rem(me * per + ahead, tiles))
-        for n, (src, dst) in enumerate(singles):
-            pltpu.make_async_copy(src.at[:, at], dst.at[c], load_sem.at[1 + n]).start()
-        return 0
-
-    lax.fori_loop(0, wins + 1, load_static, 0)
+    ends = (
+        (pl.ds(pl.multiple_of(me * share, 128), share), pl.ds(0, share)),
+        (tile(lax.rem(me * per + per, tiles)), pl.ds(share, 128)),
+        (tile(lax.rem(me * per + tiles - 1, tiles)), pl.ds(share + 128, 128)),
+    )
+    for n, (src, dst) in enumerate(singles):
+        for there, here in ends:
+            pltpu.make_async_copy(src.at[:, there], dst.at[:, here], load_sem.at[1 + n]).start()
+    table = row_table.at[:, pl.ds(pl.multiple_of(band * rows, 8), tall), :]
+    pltpu.make_async_copy(table, rows_in, load_sem.at[5]).start()
 
     barrier = pltpu.get_barrier_semaphore()
     for i in range(1, sections):
@@ -74,25 +67,26 @@
         )
     pl.semaphore_wait(barrier, sections + bands - 2)
 
-    loaded = wide.at[pl.ds(0, tiles)]
-    pltpu.make_async_copy(loaded, loaded, load_sem.at[0]).wait()
+    pltpu.make_async_copy(states, plain, load_sem.at[0]).wait()
     early = lax.broadcasted_iota(jnp.int32, (8, 128), 1) < 64
 
-    def pack(r, _):
-        at = pl.ds(pl.multiple_of(8 * r, 8), 8)
-        for j in range(sections):
-            after, before = (j + 1) % sections * wins, (j - 1) % sections * wins + per - 1
+    def pack(j, write):
+        def body(r, _):
+            r0 = pl.multiple_of(8 * r, 8)
+            at = pl.ds(r0, 8)
             for a in range(3):
-                wide[j * wins + per, a, at, :] = jnp.where(
-                    early, wide[after, a, at, :], wide[before, a, at, :]
-                )
-        return 0
-
-    lax.fori_loop(0, rows // 8, pack, 0)
+                for c in range(per):
+                    write(c, a, r0, plain[a, at, tile(j * per + c)])
+                after = plain[a, at, tile(lax.rem(j * per + per, tiles))]
+                before = plain[a, at, tile(lax.rem(j * per + tiles - 1, tiles))]
+                write(per, a, r0, jnp.where(early, after, before))
+            return 0
+
+        lax.fori_loop(0, rows // 8, body, 0)
 
     def piece(j, slot):
         return pltpu.make_async_remote_copy(
-            src_ref=wide.at[pl.ds(j * wins, wins)],
+            src_ref=wide.at[j],
             dst_ref=start.at[me, :, :, pl.ds(top, rows), :],
             send_sem=s1.at[j],
             recv_sem=r1.at[slot],
@@ -103,14 +97,26 @@
     def turn(n):
         return lax.rem(me + jnp.where(lax.rem(me, 2) == 0, n, sections - n), sections)
 
-    for n in range(1, sections - 1):
-        piece(turn(n), me).start()
-    own = pltpu.make_async_copy(
-        wide.at[pl.ds(me * wins, wins)],
-        start.at[me, :, :, pl.ds(top, rows), :],
-        own_sem.at[0],
-    )
-    own.start()
+    def pack_piece(n, _):
+        j = turn(n)
+
+        def write(c, a, r0, x):
+            wide[j, c, a, pl.ds(r0, 8), :] = x
+
+        pack(j, write)
+
+        @pl.when(n < sections - 1)
+        def _():
+            piece(j, me).start()
+
+        return 0
+
+    lax.fori_loop(1, sections, pack_piece, 0)
+
+    def write_own(c, a, r0, x):
+        start[me, c, a, pl.ds(pl.multiple_of(top + r0, 8), 8), :] = x
+
+    pack(me, write_own)
 
     up_ok, down_ok = band > 0, band < bands - 1
 
@@ -132,14 +138,14 @@
 
     def st_above():
         return pltpu.make_async_remote_copy(
-            src_ref=st.at[:, pl.ds(0, wins), pl.ds(top, HALO), :], dst_ref=st.at[:, pl.ds(0, wins), pl.ds(low, HALO), :],
+            src_ref=st.at[:, :, pl.ds(top, HALO), :], dst_ref=st.at[:, :, pl.ds(low, HALO), :],
             send_sem=st_s.at[0], recv_sem=st_r.at[0],
             device_id={"lat": band - 1}, device_id_type=MESH,
         )
 
     def st_below():
         return pltpu.make_async_remote_copy(
-            src_ref=st.at[:, pl.ds(0, wins), pl.ds(low - HALO, HALO), :], dst_ref=st.at[:, pl.ds(0, wins), pl.ds(0, HALO), :],
+            src_ref=st.at[:, :, pl.ds(low - HALO, HALO), :], dst_ref=st.at[:, :, pl.ds(0, HALO), :],
             send_sem=st_s.at[1], recv_sem=st_r.at[1],
             device_id={"lat": band + 1}, device_id_type=MESH,
         )
@@ -162,20 +168,26 @@
         def _():
             to_below(s).wait_recv()
 
-    own.wait()
     send_halo(me)
 
     for n, (src, dst) in enumerate(singles):
         pltpu.make_async_copy(dst, dst, load_sem.at[1 + n]).wait()
 
     def prepare(r, _):
-        at = pl.ds(pl.multiple_of(top + 8 * r, 8), 8)
-        for c in range(wins + 1):
-            sea = mask_win[c, pl.ds(pl.multiple_of(8 * r, 8), 8), :].astype(jnp.float32)
-            st[1, c, at, :] = sea
-            st[0, c, at, :] = st[0, c, at, :] * sea
-        for a in range(4):
-            st[a, per, at, :] = jnp.where(early, st[a, per, at, :], st[a, wins, at, :])
+        r0 = pl.multiple_of(8 * r, 8)
+        at, to = pl.ds(r0, 8), pl.ds(pl.multiple_of(top + r0, 8), 8)
+        for c in range(wins):
+            def window(ref):
+                x = ref[at, c * 128 : c * 128 + 128]
+                if c == per:
+                    x = jnp.where(early, x, ref[at, c * 128 + 128 : c * 128 + 256])
+                return x.astype(jnp.float32)
+
+            sea = window(plain_mask)
+            st[0, c, to, :] = window(plain_st.at[0]) * sea
+            st[1, c, to, :] = sea
+            st[2, c, to, :] = window(plain_st.at[1])
+            st[3, c, to, :] = window(plain_st.at[2])
         return 0
 
     lax.fori_loop(0, rows // 8, prepare, 0)
@@ -218,6 +230,7 @@
                 buf[c, pl.ds(8 * hi + 8, 8), :] = zero
 
     acc[...] = jnp.zeros_like(acc)
+    pltpu.make_async_copy(table, rows_in, load_sem.at[5]).wait()
 
     @pl.when(down_ok)
     def _():
@@ -339,6 +352,33 @@
         piece(s, s).wait_recv()
         send_halo(s)
 
+    def subtract(s, first_strip, last_strip):
+        after = lax.rem(s + 1, sections)
+        at = pl.ds(8 * first_strip, 8 * (last_strip - first_strip))
+
+        def body(c, _):
+            for a in range(3):
+                mis[s, c, a, at, :] = mis[s, c, a, at, :] - start[after, c, a, at, :]
+            return 0
+
+        lax.fori_loop(0, wins, body, 0)
+
+    columns = pl.ds(me * per, per)
+
+    def give(source, target, send, recv, s, at_columns, slot):
+        return pltpu.make_async_remote_copy(
+            src_ref=source.at[s, pl.ds(0, per), :, pl.ds(top, rows), :],
+            dst_ref=target.at[at_columns],
+            send_sem=send.at[s], recv_sem=recv.at[slot],
+            device_id={"sec": s}, device_id_type=MESH,
+        )
+
+    def send_mismatch(n):
+        subtract(turn(n), top // 8, low // 8)
+        give(mis, home, s2, r2, turn(n), columns, me).start()
+
+    even = lax.rem(me, 2) == 0
+
     def forced(n, _):
         @pl.when(n == 1)
         def _():
@@ -348,33 +388,28 @@
             for i in range(1, sections - 1):
                 arrive(i)
 
-        @pl.when(n == sections - 2)
-        def _():
-            arrive(sections - 1)
-
         s = turn(n)
         recv_halo(s)
         run("forced", start, s, 0, strips, keep, (mis, s))
+
+        late = jnp.logical_and(n == sections - 2, even)
+
+        @pl.when(jnp.logical_and(n > 0, jnp.logical_not(late)))
+        def _():
+            send_mismatch(n)
+
+        @pl.when(n == sections - 2)
+        def _():
+            arrive(sections - 1)
+
+        @pl.when(late)
+        def _():
+            send_mismatch(n)
+
         return 0
 
     lax.fori_loop(0, sections, forced, 0)
-
-    def subtract(s, after):
-        def body(r, _):
-            at = pl.ds(pl.multiple_of(8 * r, 8), 8)
-            out = [
-                [mis[s, c, a, at, :] - start[after, c, a, at, :] for a in range(3)]
-                for c in range(wins)
-            ]
-            for c in range(wins):
-                for a in range(3):
-                    mis[s, c, a, at, :] = out[c][a]
-            return 0
-
-        lax.fori_loop(1, strips - 1, body, 0)
-
-    subtract(me, peer(1))
-    columns = pl.ds(me * per, per)
+    subtract(me, top // 8, low // 8)
     own_mis = pltpu.make_async_copy(
         mis.at[me, pl.ds(0, per), :, pl.ds(top, rows), :],
         home.at[columns],
@@ -382,25 +417,16 @@
     )
     own_mis.start()
 
-    def give(source, target, send, recv, s, at_columns, slot):
-        return pltpu.make_async_remote_copy(
-            src_ref=source.at[s, pl.ds(0, per), :, pl.ds(top, rows), :],
-            dst_ref=target.at[at_columns],
-            send_sem=send.at[s], recv_sem=recv.at[slot],
-            device_id={"sec": s}, device_id_type=MESH,
-        )
-
-    def differ(i, _):
-        s = peer(i)
-        subtract(s, peer(i + 1))
-        give(mis, home, s2, r2, s, columns, me).start()
-        return 0
-
-    lax.fori_loop(1, sections, differ, 0)
+    def fringe(s, _):
+        subtract(s, 1, top // 8)
+        subtract(s, low // 8, strips - 1)
+        return 0
+
+    lax.fori_loop(0, sections, fringe, 0)
 
     def back(i, _):
-        s = peer(i)
-        before = peer(i + sections - 1)
+        s = turn(lax.rem(i, sections))
+        before = lax.rem(s + sections - 1, sections)
 
         def done(c, at, values):
             return [x - mis[before, c, a, at, :] for a, x in enumerate(values)]
@@ -528,12 +554,12 @@
 
 
 def finish_kernel(fields, home, full, step, new_fields, mismatch):
-    rows, share = fields.shape[1:]
+    rows, width = fields.shape[1:]
     length = step[0:1, :]
 
     def body(r, _):
         at = pl.ds(pl.multiple_of(8 * r, 8), 8)
-        for c in range(share // 128):
+        for c in range(width // 128):
             cols = slice(c * 128, c * 128 + 128)
             for a in range(3):
                 new_fields[a, at, cols] = fields[a, at, cols] - length * full[c, a, at, :]
@@ -547,16 +573,15 @@
     fields = states[0]
     rows, lon = fields.shape[1:]
     sections, bands = lax.axis_size("sec"), lax.axis_size("lat")
-    band = lax.axis_index("lat")
     share = lon // sections
     tall = rows + 2 * HALO
     lat_total = rows * bands
-    ids = band * rows - HALO + jnp.arange(tall, dtype=jnp.int32)
-    inside = ((ids >= 0) & (ids < lat_total)).astype(jnp.float32)
-    coriolis = CORIOLIS_MAX * jnp.sin(
-        jnp.pi * (ids.astype(jnp.float32) + 0.5) / lat_total - 0.5 * jnp.pi
-    )
-    rows_in = jnp.broadcast_to(jnp.stack([coriolis, inside])[:, :, None], (2, tall, 128))
+    ids = np.arange(lat_total + 2 * HALO, dtype=np.float32) - HALO
+    inside = ((ids >= 0) & (ids < lat_total)).astype(np.float32)
+    turned = np.float32(math.pi) * (ids + np.float32(0.5)) / np.float32(lat_total)
+    coriolis = np.float32(CORIOLIS_MAX) * np.sin(turned - np.float32(0.5 * math.pi))
+    row_table = np.broadcast_to(np.stack([coriolis, inside])[:, :, None], (2, ids.size, 128))
+    row_table = jnp.asarray(row_table.astype(np.float32))
     angles = np.float32(TWO_PI) * np.arange(sections * STEPS, dtype=np.float32) / np.float32(
         sections * STEPS
     )
@@ -577,18 +602,21 @@
             gathered,
             jax.ShapeDtypeStruct((8, 128), f32),
         ),
-        in_specs=[any_spec] * 5 + [vmem, pl.BlockSpec(memory_space=pltpu.SMEM)],
+        in_specs=[any_spec] * 6 + [pl.BlockSpec(memory_space=pltpu.SMEM)],
         out_specs=(any_spec, any_spec, vmem),
         scratch_shapes=[
-            pltpu.VMEM((tiles + sections, 3, rows, 128), f32),
-            pltpu.VMEM((wins + 1, rows, 128), jnp.int32),
-            pltpu.VMEM((4, wins + 1, tall, 128), f32),
+            pltpu.VMEM((3, rows, lon), f32),
+            pltpu.VMEM((3, rows, share + 256), f32),
+            pltpu.VMEM((rows, share + 256), jnp.int32),
+            pltpu.VMEM((2, tall, 128), f32),
+            pltpu.VMEM((sections, wins, 3, rows, 128), f32),
+            pltpu.VMEM((4, wins, tall, 128), f32),
             stacked, stacked, stacked,
             plain, plain, plain, padded, padded, plain,
             pltpu.VMEM((2, 8, 128), f32),
             pltpu.VMEM((sections, 2, 8, 128), f32),
             pltpu.VMEM((bands, 2, 8, 128), f32),
-            dma((5,)),
+            dma((6,)),
             dma((sections,)), dma((sections,)),
             dma((2, sections)), dma((2, sections)),
             dma((2,)), dma((2,)),
@@ -602,16 +630,17 @@
             collective_id=0, has_side_effects=True, vmem_limit_bytes=60 * 1024 * 1024
         ),
         name="shooting",
-    )(fields, depth_field, land_mask, tide_cos, tide_sin, rows_in, trig)
-    block = pl.BlockSpec((3, rows, share), lambda i: (0, 0, i))
-    by_tile = pl.BlockSpec((share // 128, 3, rows, 128), lambda i: (i, 0, 0, 0))
+    )(fields, depth_field, land_mask, tide_cos, tide_sin, row_table, trig)
+    half = share // 2
+    block = pl.BlockSpec((3, rows, half), lambda i: (0, 0, i))
+    by_tile = pl.BlockSpec((half // 128, 3, rows, 128), lambda i: (i, 0, 0, 0))
     new_fields, mismatch = pl.pallas_call(
         finish_kernel,
-        grid=(sections,),
+        grid=(2 * sections,),
         out_shape=(jax.ShapeDtypeStruct(fields.shape, f32),) * 2,
         in_specs=[block, by_tile, by_tile, pl.BlockSpec((8, 128), lambda i: (0, 0))],
         out_specs=(block, block),
-        compiler_params=pltpu.CompilerParams(vmem_limit_bytes=32 * 1024 * 1024),
+        compiler_params=pltpu.CompilerParams(vmem_limit_bytes=60 * 1024 * 1024),
         name="update",
     )(fields, home, full, step)
     return new_fields[None], mismatch[None], step[0, 0]

time: 126 us -> 119 us (0.944); the launches traced: 126 us -> 117 us
  local copies, waits for them, and re-layouts: 5.49 us -> 1.18 us
  Pallas kernels: 119 us -> 115 us
    pallas_call x1, Pallas kernels: 116 us -> 107 us  [shards(): pl.pallas_call(functools.partial(kernel, sections, bands, float(sections...]
    pallas_call x1, Pallas kernels: 3.07 us -> 7.99 us  [shards(): pl.pallas_call(finish_kernel, grid=(2 * sections,), out_shape=(jax.ShapeD...]
    unnamed x8 -> x0, local copies, waits for them, and re-layouts: 4.24 us -> none
where the time goes in v1:
time: 119 us; the launch traced here: 117 us
  Pallas kernels  115 us (97%)
    pallas_call x1, Pallas kernels, shards(): pl.pallas_call(functools.partial(kernel, sections, bands, float(sections...  107 us
    pallas_call x1, Pallas kernels, shards(): pl.pallas_call(finish_kernel, grid=(2 * sections,), out_shape=(jax.ShapeD...  7.99 us

profile of v1, /device:TPU:0, one launch (start us, length us, event | category | flops | bytes accessed | tf_op | source)
XLA Modules:
  0.0 117.1 jit_solution(3403284891270062105)
XLA Ops:
  0.6 107.3 %shooting.1 = (f32[32,3,56,128]{3,2,1,0:T(8,128)}, f32[32,3,56,128]{3,2,1,0:T(8,128)}, f32[8,128]{1,0:T(8,128)}) custom-call(f32[3,56,4096]{2,1,0:T(8,128)} %bitcast.4, f32[56,4096]{1,0:T(8,128)} %depth.1, s32[56,4096]{1,0:T(8,128)} %mask.1, f32[56,4096]{1,0:T(8,128)} %tide_one.1, f32[56,4096]{1,0:T(8,128)} %tide_two.1, ...), custom_call_target="tpu_custom_call" | custom-call | tf_op jit(solution)/shard_map/shooting/pallas_call | solution.py:598
  107.9 8.0 %update.1 = (f32[3,56,4096]{2,1,0:T(8,128)}, f32[3,56,4096]{2,1,0:T(8,128)}) custom-call(f32[3,56,4096]{2,1,0:T(8,128)} %bitcast.5, f32[32,3,56,128]{3,2,1,0:T(8,128)} %get-tuple-element.8.home, f32[32,3,56,128]{3,2,1,0:T(8,128)} %get-tuple-element.9.full, f32[8,128]{1,0:T(8,128)} %get-tuple-element.10.step), custom_call_target="tpu_custom_call" | custom-call | tf_op jit(solution)/shard_map/update/pallas_call | solution.py:637
  115.9 1.2 %slice.3 = f32[1,1]{1,0:T(1,128)} slice(f32[8,128]{1,0:T(8,128)} %get-tuple-element.10.step), slice={[0:1], [0:1]} | slice | bytes 8 | tf_op jit(solution)/shard_map/slice | solution.py:646

commit v2 on v1

--- a/solution.py
+++ b/solution.py
@@ -43,6 +43,13 @@
     def tile(c):
         return pl.ds(pl.multiple_of(c * 128, 128), 128)
 
+    barrier = pltpu.get_barrier_semaphore()
+    for i in range(1, sections):
+        pl.semaphore_signal(barrier, inc=1, device_id={"sec": peer(i)}, device_id_type=MESH)
+    for i in range(1, bands):
+        pl.semaphore_signal(
+            barrier, inc=1, device_id={"lat": lax.rem(band + i, bands)}, device_id_type=MESH
+        )
     pltpu.make_async_copy(states, plain, load_sem.at[0]).start()
     singles = (
         (depth, plain_st.at[0]), (mask, plain_mask), (tide_one, plain_st.at[1]), (tide_two, plain_st.at[2])
@@ -58,15 +65,6 @@
     table = row_table.at[:, pl.ds(pl.multiple_of(band * rows, 8), tall), :]
     pltpu.make_async_copy(table, rows_in, load_sem.at[5]).start()
 
-    barrier = pltpu.get_barrier_semaphore()
-    for i in range(1, sections):
-        pl.semaphore_signal(barrier, inc=1, device_id={"sec": peer(i)}, device_id_type=MESH)
-    for i in range(1, bands):
-        pl.semaphore_signal(
-            barrier, inc=1, device_id={"lat": lax.rem(band + i, bands)}, device_id_type=MESH
-        )
-    pl.semaphore_wait(barrier, sections + bands - 2)
-
     pltpu.make_async_copy(states, plain, load_sem.at[0]).wait()
     early = lax.broadcasted_iota(jnp.int32, (8, 128), 1) < 64
 
@@ -104,11 +102,6 @@
             wide[j, c, a, pl.ds(r0, 8), :] = x
 
         pack(j, write)
-
-        @pl.when(n < sections - 1)
-        def _():
-            piece(j, me).start()
-
         return 0
 
     lax.fori_loop(1, sections, pack_piece, 0)
@@ -117,6 +110,10 @@
         start[me, c, a, pl.ds(pl.multiple_of(top + r0, 8), 8), :] = x
 
     pack(me, write_own)
+    pl.semaphore_wait(barrier, sections + bands - 2)
+
+    for n in range(1, sections - 1):
+        piece(turn(n), me).start()
 
     up_ok, down_ok = band > 0, band < bands - 1
 
@@ -383,10 +380,10 @@
         @pl.when(n == 1)
         def _():
             for i in range(1, sections - 1):
+                arrive(i)
+            for i in range(1, sections - 1):
                 piece(turn(i), me).wait_send()
             piece(turn(sections - 1), me).start()
-            for i in range(1, sections - 1):
-                arrive(i)
 
         s = turn(n)
         recv_halo(s)
@@ -460,25 +457,7 @@
 
     lax.fori_loop(0, sections, image, 0)
 
-    part[me] = acc[...]
-
-    def share_part(j, slot):
-        return pltpu.make_async_remote_copy(
-            src_ref=acc, dst_ref=part.at[slot], send_sem=ps.at[j], recv_sem=pr.at[slot],
-            device_id={"sec": j}, device_id_type=MESH,
-        )
-
-    for i in range(1, sections):
-        share_part(peer(i), me).start()
-    for i in range(1, sections):
-        share_part(peer(i), peer(i)).wait_recv()
-    for i in range(1, sections):
-        share_part(peer(i), me).wait_send()
-    summed = part[0]
-    for s in range(1, sections):
-        summed = summed + part[s]
-    acc[...] = summed
-    total[band] = summed
+    total[band] = acc[...]
 
     def share_total(j, slot):
         return pltpu.make_async_remote_copy(
@@ -491,9 +470,32 @@
     for i in range(1, bands):
         j = lax.rem(band + i, bands)
         share_total(j, j).wait_recv()
+    for i in range(1, bands):
+        share_total(lax.rem(band + i, bands), band).wait_send()
     summed = total[0]
     for s in range(1, bands):
         summed = summed + total[s]
+    acc[...] = summed
+    part[me] = summed
+
+    def share_part(j, slot):
+        return pltpu.make_async_remote_copy(
+            src_ref=acc, dst_ref=part.at[slot], send_sem=ps.at[j], recv_sem=pr.at[slot],
+            device_id={"sec": j}, device_id_type=MESH,
+        )
+
+    for i in range(1, sections):
+        share_part(peer(i), me).start()
+
+    def rest(n, _):
+        give(grad, full, s3, r3, turn(n), columns, me).start()
+        return 0
+
+    for i in range(1, sections):
+        share_part(peer(i), peer(i)).wait_recv()
+    summed = part[0]
+    for s in range(1, sections):
+        summed = summed + part[s]
     sums = jnp.sum(jnp.sum(summed, axis=2, keepdims=True), axis=1, keepdims=True)
     step = sums[0] / count / (sums[1] / count + EPSILON)
     step_out[...] = jnp.broadcast_to(step, (8, 128))
@@ -549,13 +551,14 @@
     def _():
         st_below().wait_send()
 
-    for i in range(1, bands):
-        share_total(lax.rem(band + i, bands), band).wait_send()
-
-
-def finish_kernel(fields, home, full, step, new_fields, mismatch):
+    for i in range(1, sections):
+        share_part(peer(i), me).wait_send()
+
+
+def finish_kernel(fields, home, full, step, new_fields, mismatch, step_out):
     rows, width = fields.shape[1:]
     length = step[0:1, :]
+    step_out[0, 0] = step[0, 0]
 
     def body(r, _):
         at = pl.ds(pl.multiple_of(8 * r, 8), 8)
@@ -631,19 +634,19 @@
         ),
         name="shooting",
     )(fields, depth_field, land_mask, tide_cos, tide_sin, row_table, trig)
-    half = share // 2
+    half = 2 * share
     block = pl.BlockSpec((3, rows, half), lambda i: (0, 0, i))
     by_tile = pl.BlockSpec((half // 128, 3, rows, 128), lambda i: (i, 0, 0, 0))
-    new_fields, mismatch = pl.pallas_call(
+    new_fields, mismatch, length = pl.pallas_call(
         finish_kernel,
-        grid=(2 * sections,),
-        out_shape=(jax.ShapeDtypeStruct(fields.shape, f32),) * 2,
+        grid=(sections // 2,),
+        out_shape=(jax.ShapeDtypeStruct(fields.shape, f32),) * 2 + (jax.ShapeDtypeStruct((1, 1), f32),),
         in_specs=[block, by_tile, by_tile, pl.BlockSpec((8, 128), lambda i: (0, 0))],
-        out_specs=(block, block),
+        out_specs=(block, block, pl.BlockSpec(memory_space=pltpu.SMEM)),
         compiler_params=pltpu.CompilerParams(vmem_limit_bytes=60 * 1024 * 1024),
         name="update",
     )(fields, home, full, step)
-    return new_fields[None], mismatch[None], step[0, 0]
+    return new_fields[None], mismatch[None], length.reshape(())
 
 
 def solution(mesh):

time: 119 us -> 112 us (0.941); the launches traced: 117 us -> 112 us
  Pallas kernels: 115 us -> 111 us
    pallas_call x1, Pallas kernels: 7.99 us -> 5.26 us  [shards(): pl.pallas_call(finish_kernel, grid=(sections // 2,), out_shape=(jax.Shape...]
    pallas_call x1, Pallas kernels: 107 us -> 106 us  [shards(): pl.pallas_call(functools.partial(kernel, sections, bands, float(sections...]
where the time goes in v2:
time: 112 us
  Pallas kernels  111 us (99%)
    pallas_call x1, Pallas kernels, shards(): pl.pallas_call(functools.partial(kernel, sections, bands, float(sections...  106 us
    pallas_call x1, Pallas kernels, shards(): pl.pallas_call(finish_kernel, grid=(sections // 2,), out_shape=(jax.Shape...  5.26 us

profile of v2, /device:TPU:0, one launch (start us, length us, event | category | flops | bytes accessed | tf_op | source)
XLA Modules:
  0.0 111.7 jit_solution(969572625751887784)
XLA Ops:
  0.6 105.8 %shooting.1 = (f32[32,3,56,128]{3,2,1,0:T(8,128)}, f32[32,3,56,128]{3,2,1,0:T(8,128)}, f32[8,128]{1,0:T(8,128)}) custom-call(f32[3,56,4096]{2,1,0:T(8,128)} %bitcast.4, f32[56,4096]{1,0:T(8,128)} %depth.1, s32[56,4096]{1,0:T(8,128)} %mask.1, f32[56,4096]{1,0:T(8,128)} %tide_one.1, f32[56,4096]{1,0:T(8,128)} %tide_two.1, ...), custom_call_target="tpu_custom_call" | custom-call | tf_op jit(solution)/shard_map/shooting/pallas_call | solution.py:601
  106.5 5.3 %update.1 = (f32[3,56,4096]{2,1,0:T(8,128)}, f32[3,56,4096]{2,1,0:T(8,128)}, f32[1,1]{1,0:T(1,128)}) custom-call(f32[3,56,4096]{2,1,0:T(8,128)} %bitcast.5, f32[32,3,56,128]{3,2,1,0:T(8,128)} %get-tuple-element.9.home, f32[32,3,56,128]{3,2,1,0:T(8,128)} %get-tuple-element.10.full, f32[8,128]{1,0:T(8,128)} %get-tuple-element.11.step), custom_call_target="tpu_custom_call" | custom-call | tf_op jit(solution)/shard_map/update/pallas_call | solution.py:640

commit v3 on v2

--- a/solution.py
+++ b/solution.py
@@ -112,7 +112,7 @@
     pack(me, write_own)
     pl.semaphore_wait(barrier, sections + bands - 2)
 
-    for n in range(1, sections - 1):
+    for n in range(1, sections):
         piece(turn(n), me).start()
 
     up_ok, down_ok = band > 0, band < bands - 1
@@ -383,7 +383,6 @@
                 arrive(i)
             for i in range(1, sections - 1):
                 piece(turn(i), me).wait_send()
-            piece(turn(sections - 1), me).start()
 
         s = turn(n)
         recv_halo(s)

time: 112 us -> 110 us (0.982)
    pallas_call x1, Pallas kernels: 106 us -> 104 us  [shards(): pl.pallas_call(functools.partial(kernel, sections, bands, float(sections...]
where the time goes in v3:
time: 110 us
  Pallas kernels  110 us (100%)
    pallas_call x1, Pallas kernels, shards(): pl.pallas_call(functools.partial(kernel, sections, bands, float(sections...  104 us
    pallas_call x1, Pallas kernels, shards(): pl.pallas_call(finish_kernel, grid=(sections // 2,), out_shape=(jax.Shape...  5.26 us

profile of v3, /device:TPU:0, one launch (start us, length us, event | category | flops | bytes accessed | tf_op | source)
XLA Modules:
  0.0 110.3 jit_solution(14390605520117124380)
XLA Ops:
  0.6 104.4 %shooting.1 = (f32[32,3,56,128]{3,2,1,0:T(8,128)}, f32[32,3,56,128]{3,2,1,0:T(8,128)}, f32[8,128]{1,0:T(8,128)}) custom-call(f32[3,56,4096]{2,1,0:T(8,128)} %bitcast.4, f32[56,4096]{1,0:T(8,128)} %depth.1, s32[56,4096]{1,0:T(8,128)} %mask.1, f32[56,4096]{1,0:T(8,128)} %tide_one.1, f32[56,4096]{1,0:T(8,128)} %tide_two.1, ...), custom_call_target="tpu_custom_call" | custom-call | tf_op jit(solution)/shard_map/shooting/pallas_call | solution.py:600
  105.0 5.3 %update.1 = (f32[3,56,4096]{2,1,0:T(8,128)}, f32[3,56,4096]{2,1,0:T(8,128)}, f32[1,1]{1,0:T(1,128)}) custom-call(f32[3,56,4096]{2,1,0:T(8,128)} %bitcast.5, f32[32,3,56,128]{3,2,1,0:T(8,128)} %get-tuple-element.9.home, f32[32,3,56,128]{3,2,1,0:T(8,128)} %get-tuple-element.10.full, f32[8,128]{1,0:T(8,128)} %get-tuple-element.11.step), custom_call_target="tpu_custom_call" | custom-call | tf_op jit(solution)/shard_map/update/pallas_call | solution.py:639

commit v4 on v3

--- a/solution.py
+++ b/solution.py
@@ -112,8 +112,11 @@
     pack(me, write_own)
     pl.semaphore_wait(barrier, sections + bands - 2)
 
+    def order(n):
+        return jnp.where(jnp.logical_and(lax.rem(band, 2) == 1, n < 3), 3 - n, n)
+
     for n in range(1, sections):
-        piece(turn(n), me).start()
+        piece(turn(order(n)), me).start()
 
     up_ok, down_ok = band > 0, band < bands - 1
 
@@ -421,7 +424,7 @@
     lax.fori_loop(0, sections, fringe, 0)
 
     def back(i, _):
-        s = turn(lax.rem(i, sections))
+        s = turn(lax.rem(jnp.where(i < sections, order(i), i), sections))
         before = lax.rem(s + sections - 1, sections)
 
         def done(c, at, values):

time: 110 us -> 110 us (level)
  no operation moved by 1% of the time
where the time goes in v4:
time: 110 us
  Pallas kernels  110 us (100%)
    pallas_call x1, Pallas kernels, shards(): pl.pallas_call(functools.partial(kernel, sections, bands, float(sections...  104 us
    pallas_call x1, Pallas kernels, shards(): pl.pallas_call(finish_kernel, grid=(sections // 2,), out_shape=(jax.Shape...  5.26 us

profile of v4, /device:TPU:0, one launch (start us, length us, event | category | flops | bytes accessed | tf_op | source)
XLA Modules:
  0.0 110.3 jit_solution(2418701588369054889)
XLA Ops:
  0.6 104.4 %shooting.1 = (f32[32,3,56,128]{3,2,1,0:T(8,128)}, f32[32,3,56,128]{3,2,1,0:T(8,128)}, f32[8,128]{1,0:T(8,128)}) custom-call(f32[3,56,4096]{2,1,0:T(8,128)} %bitcast.4, f32[56,4096]{1,0:T(8,128)} %depth.1, s32[56,4096]{1,0:T(8,128)} %mask.1, f32[56,4096]{1,0:T(8,128)} %tide_one.1, f32[56,4096]{1,0:T(8,128)} %tide_two.1, ...), custom_call_target="tpu_custom_call" | custom-call | tf_op jit(solution)/shard_map/shooting/pallas_call | solution.py:603
  105.0 5.3 %update.1 = (f32[3,56,4096]{2,1,0:T(8,128)}, f32[3,56,4096]{2,1,0:T(8,128)}, f32[1,1]{1,0:T(1,128)}) custom-call(f32[3,56,4096]{2,1,0:T(8,128)} %bitcast.5, f32[32,3,56,128]{3,2,1,0:T(8,128)} %get-tuple-element.9.home, f32[32,3,56,128]{3,2,1,0:T(8,128)} %get-tuple-element.10.full, f32[8,128]{1,0:T(8,128)} %get-tuple-element.11.step), custom_call_target="tpu_custom_call" | custom-call | tf_op jit(solution)/shard_map/update/pallas_call | solution.py:642
